TPU v7x, 512 devices: a whole 4x4x16 slice. The times are simulated.
512 devices in a mesh: ctx: 64 (over y, z), uly: 8 (over x, core).
Axes of the slice: x: 4, y: 4, z: 16, core: 2. Of those that a mesh axis runs over, the one named last changes fastest.
Arguments:
- lin_query: bfloat16 [32768, 4096], P(('ctx', 'uly')), may hold values from -5 to 5
- lin_key: bfloat16 [32768, 4096], P(('ctx', 'uly')), may hold values from -5 to 5
- lin_value: bfloat16 [32768, 4096], P(('ctx', 'uly')), may hold values from -60 to 60
- log_decay: bfloat16 [32768, 32], P(('ctx', 'uly')), may hold values from 0 to 1
- norm_gain: float32 [4096], P('uly'), may hold values from 0.25 to 1.75
- doc_lengths: int32 [64], replicated, may hold values from 1 to 1024, 32768 in all
- att_query: bfloat16 [32768, 4096], P(('ctx', 'uly')), may hold values from -6 to 6
- att_key: bfloat16 [32768, 1024], P(('ctx', 'uly')), may hold values from -6 to 6
- att_value: bfloat16 [32768, 1024], P(('ctx', 'uly')), may hold values from -5 to 5
Outputs:
- lin_out: bfloat16 [32768, 4096], P('ctx', 'uly')
- att_out: bfloat16 [32768, 4096], P('ctx', 'uly')
Inputs may be any that keep to these rules, and one draw needn't show every extreme that they name: `doc_lengths`: documents follow one another from position 0 and fill the sequence; the longest has exactly 1024 positions.
All inputs are finite; a program needn't handle non-finite values.
Results may differ from a plain program's by a relative error of at most 0.008.
Values may be sent and summed in bfloat16 or wider, within the bound.
No kernel may reach another device: no remote copies, remote signals or barrier semaphores. Data moves between devices by JAX's collectives and lax.ppermute only.
A program may use at most 128 MiB of HBM per device.

v0:
```python
import jax
import jax.numpy as jnp
from jax import lax
from jax.sharding import PartitionSpec as P

HEAD = 128
WIN = 2


def prefix(x, axis, join, neutral):
    place = lax.axis_index(axis)
    gathered = jax.tree.map(
        lambda a, kind: lax.all_gather(a.astype(kind), axis), x, (jnp.bfloat16, jnp.bfloat16)
    )
    state = jax.tree.map(lambda a, e: jnp.zeros_like(a) + jnp.asarray(e, a.dtype), x, neutral)

    def one(turn, state):
        return join(
            state,
            jax.tree.map(
                lambda a, own: lax.dynamic_index_in_dim(a, turn, 0, False).astype(own.dtype),
                gathered,
                x,
            ),
        )

    return lax.fori_loop(0, place, one, state)


def shifted(block, axis, distance):
    devices = range(lax.axis_size(axis))
    route = [(i - distance, i) for i in devices if i - distance in devices]
    return lax.ppermute(block, axis, route)


def doc_begin(positions, doc_lengths):
    start_pos = jnp.cumsum(doc_lengths) - doc_lengths
    covered = start_pos[None, :] <= positions[:, None]
    return jnp.max(jnp.where(covered, start_pos[None, :], 0), axis=1)


def combine_states(earlier, later_part):
    return (earlier[0] * later_part[0], later_part[0][:, None, None] * earlier[1] + later_part[1])


def shards(
    lin_query, lin_key, lin_value, log_decay, norm_gain, doc_lengths, att_query, att_key, att_value
):
    query_in, key_in, value_in, decay_in, att_q, att_k, att_v = (
        lax.all_to_all(lin_query, "uly", split_axis=1, concat_axis=0, tiled=True),
        lax.all_to_all(lin_key, "uly", split_axis=1, concat_axis=0, tiled=True),
        lax.all_to_all(lin_value, "uly", split_axis=1, concat_axis=0, tiled=True),
        lax.all_to_all(log_decay, "uly", split_axis=1, concat_axis=0, tiled=True),
        lax.all_to_all(att_query, "uly", split_axis=1, concat_axis=0, tiled=True),
        lax.all_to_all(att_key, "uly", split_axis=1, concat_axis=0, tiled=True),
        lax.all_to_all(att_value, "uly", split_axis=1, concat_axis=0, tiled=True),
    )
    block_len = query_in.shape[0]
    head_count = decay_in.shape[1]
    block_start = lax.axis_index("ctx") * block_len
    offsets = jnp.arange(block_len, dtype=jnp.int32)
    positions = block_start + offsets
    token_begin = doc_begin(positions, doc_lengths)
    decay_sum = jnp.cumsum(decay_in.astype(jnp.float32), axis=0)
    query_map = jax.nn.silu(
        query_in.reshape(block_len, head_count, HEAD).astype(jnp.float32)
    ).astype(jnp.bfloat16)
    key_map = jax.nn.silu(key_in.reshape(block_len, head_count, HEAD).astype(jnp.float32)).astype(
        jnp.bfloat16
    )
    values = value_in.reshape(block_len, head_count, HEAD)
    scores = jnp.einsum("thd,shd->hts", query_map, key_map, preferred_element_type=jnp.float32)
    same_doc = (offsets[None, :] <= offsets[:, None]) & (
        token_begin[None, :] == token_begin[:, None]
    )
    decay_gap = decay_sum.T[:, :, None] - decay_sum.T[:, None, :]
    weights = jnp.where(same_doc[None], jnp.exp(-jnp.where(same_doc[None], decay_gap, 0.0)), 0.0)
    weighted_scores = (weights * scores).astype(jnp.bfloat16)
    inside = jnp.einsum("hts,shd->thd", weighted_scores, values, preferred_element_type=jnp.float32)
    last_begin = token_begin[block_len - 1]
    end_weight = jnp.where(
        (token_begin == last_begin)[:, None],
        jnp.exp(decay_sum - decay_sum[block_len - 1][None, :]),
        0.0,
    )
    end_keys = (key_map.astype(jnp.float32) * end_weight[:, :, None]).astype(jnp.bfloat16)
    end_state = jnp.einsum("shd,she->hde", end_keys, values, preferred_element_type=jnp.float32)
    block_decay = jnp.where(last_begin < block_start, jnp.exp(-decay_sum[block_len - 1]), 0.0)
    identity = (jnp.ones_like(block_decay), jnp.zeros_like(end_state))
    _, incoming = prefix((block_decay, end_state), "ctx", combine_states, identity)
    entry_decay = jnp.where((token_begin < block_start)[:, None], jnp.exp(-decay_sum), 0.0)
    carried = (
        jnp.einsum(
            "thd,hde->the",
            query_map,
            incoming.astype(jnp.bfloat16),
            preferred_element_type=jnp.float32,
        )
        * entry_decay[:, :, None]
    )
    combined = inside + carried
    normed = (
        combined
        * lax.rsqrt(jnp.mean(combined * combined, axis=-1, keepdims=True) + 1e-06)
        * norm_gain.reshape(head_count, HEAD)
    )
    lin_out = normed.astype(jnp.bfloat16).reshape(block_len, head_count * HEAD)
    kv_heads = att_k.shape[1] // HEAD
    group_size = att_q.shape[1] // (kv_heads * HEAD)
    queries = att_q.reshape(block_len, kv_heads, group_size, HEAD)
    score_scale = HEAD ** (-0.5)

    def attend(state_carry, key_block, value_block, key_position):
        row_max, row_total, accumulated = state_carry
        key_begin = doc_begin(key_position, doc_lengths)
        allowed = (
            (key_position[None, :] <= positions[:, None])
            & (key_position[None, :] >= 0)
            & (key_begin[None, :] == token_begin[:, None])
        )
        block_scores = (
            jnp.einsum(
                "tkgd,skd->kgts",
                queries,
                key_block.reshape(block_len, kv_heads, HEAD),
                preferred_element_type=jnp.float32,
            )
            * score_scale
        )
        new_max = jnp.maximum(row_max, jnp.max(jnp.where(allowed, block_scores, -1e30), axis=-1))
        att_weights = jnp.where(allowed, jnp.exp(block_scores - new_max[..., None]), 0.0)
        shrink = jnp.exp(row_max - new_max)
        row_total = row_total * shrink + jnp.sum(att_weights, axis=-1)
        products = jnp.einsum(
            "kgts,skd->tkgd",
            att_weights.astype(jnp.bfloat16),
            value_block.reshape(block_len, kv_heads, HEAD),
            preferred_element_type=jnp.float32,
        )
        accumulated = accumulated * jnp.transpose(shrink, (2, 0, 1))[..., None] + products
        return (new_max, row_total, accumulated)

    state_carry = (
        jnp.full((kv_heads, group_size, block_len), -1e30, jnp.float32),
        jnp.zeros((kv_heads, group_size, block_len), jnp.float32),
        jnp.zeros((block_len, kv_heads, group_size, HEAD), jnp.float32),
    )
    state_carry = attend(state_carry, att_k, att_v, positions)
    for distance in range(1, WIN + 1):
        earlier_keys, earlier_values = shifted((att_k, att_v), "ctx", distance)
        key_position = positions - distance * block_len
        state_carry = attend(state_carry, earlier_keys, earlier_values, key_position)
    row_max, row_total, accumulated = state_carry
    att_out = (
        (accumulated / jnp.transpose(row_total, (2, 0, 1))[..., None])
        .astype(jnp.bfloat16)
        .reshape(block_len, kv_heads * group_size * HEAD)
    )
    return (lin_out, att_out)


def solution(mesh):
    placed = (
        P(("ctx", "uly"), None),
        P(("ctx", "uly"), None),
        P(("ctx", "uly"), None),
        P(("ctx", "uly"), None),
        P("uly"),
        P(),
        P(("ctx", "uly"), None),
        P(("ctx", "uly"), None),
        P(("ctx", "uly"), None),
    )
    return jax.shard_map(
        shards,
        mesh=mesh,
        in_specs=placed,
        out_specs=(P("ctx", "uly"), P("ctx", "uly")),
        check_vma=False,
    )
```

profile of v0, /device:TPU:510, one launch (start us, length us, event | category | flops | bytes accessed | tf_op | source)
XLA Modules:
  0.0 326.6 jit_solution(10978063020451155656)
XLA Ops:
  8.6 4.8 %all-to-all-start = ((bf16[8,2,128]{2,1,0:T(2,128)(2,1)}), bf16[8,2,128]{2,1,0:T(2,128)(2,1)S(1)}, u32[]{:S(2)}, u32[]{:S(2)}) async-start(bf16[8,2,128]{2,1,0:T(2,128)(2,1)} %reshape.440), calls=%async_computation | async-start | bytes 8192 | tf_op jit(solution)/shard_map/all_to_all | solution.py:53
  17.6 1.9 copy.240
  19.5 1.9 copy.239
  21.4 4.8 %all-to-all-start.2 = ((bf16[64,8,512]{2,0,1:T(8,128)(2,1)}), bf16[64,8,512]{2,0,1:T(8,128)(2,1)S(1)}, u32[]{:S(2)}, u32[]{:S(2)}) async-start(bf16[64,8,512]{2,0,1:T(8,128)(2,1)} %bitcast.306), calls=%async_computation.2 | async-start | bytes 1048576 | tf_op jit(solution)/shard_map/all_to_all | solution.py:51
  28.8 5.7 %all-to-all-done.2 = bf16[64,8,512]{2,0,1:T(8,128)(2,1)S(1)} async-done(((bf16[64,8,512]{2,0,1:T(8,128)(2,1)}), bf16[64,8,512]{2,0,1:T(8,128)(2,1)S(1)}, u32[]{:S(2)}, u32[]{:S(2)}) %all-to-all-start.2) | async-done | bytes 524320 | tf_op jit(solution)/shard_map/all_to_all | solution.py:51
  34.5 5.5 %all-to-all-start.3 = ((bf16[64,8,512]{2,0,1:T(8,128)(2,1)}), bf16[64,8,512]{2,0,1:T(8,128)(2,1)S(1)}, u32[]{:S(2)}, u32[]{:S(2)}) async-start(bf16[64,8,512]{2,0,1:T(8,128)(2,1)} %bitcast.305), calls=%async_computation.3 | async-start | bytes 1048576 | tf_op jit(solution)/shard_map/all_to_all | solution.py:52
  41.6 6.7 %all-to-all-done.3 = bf16[64,8,512]{2,0,1:T(8,128)(2,1)S(1)} async-done(((bf16[64,8,512]{2,0,1:T(8,128)(2,1)}), bf16[64,8,512]{2,0,1:T(8,128)(2,1)S(1)}, u32[]{:S(2)}, u32[]{:S(2)}) %all-to-all-start.3) | async-done | bytes 524320 | tf_op jit(solution)/shard_map/all_to_all | solution.py:52
  50.6 6.0 %all-to-all-start.4 = ((bf16[64,8,128]{2,0,1:T(8,128)(2,1)}), bf16[64,8,128]{2,0,1:T(8,128)(2,1)}, u32[]{:S(2)}, u32[]{:S(2)}) async-start(bf16[64,8,128]{2,0,1:T(8,128)(2,1)} %copy_bitcast_fusion.5), calls=%async_computation.4 | async-start | bytes 262144 | tf_op jit(solution)/shard_map/all_to_all | solution.py:55
  57.3 3.5 %all-to-all-done.4 = bf16[64,8,128]{2,0,1:T(8,128)(2,1)} async-done(((bf16[64,8,128]{2,0,1:T(8,128)(2,1)}), bf16[64,8,128]{2,0,1:T(8,128)(2,1)}, u32[]{:S(2)}, u32[]{:S(2)}) %all-to-all-start.4) | async-done | bytes 131104 | tf_op jit(solution)/shard_map/all_to_all | solution.py:55
  60.7 5.4 %all-to-all-start.6 = ((bf16[64,8,128]{2,0,1:T(8,128)(2,1)}), bf16[64,8,128]{2,0,1:T(8,128)(2,1)S(1)}, u32[]{:S(2)}, u32[]{:S(2)}) async-start(bf16[64,8,128]{2,0,1:T(8,128)(2,1)} %copy_bitcast_fusion.4), calls=%async_computation.6 | async-start | bytes 262144 | tf_op jit(solution)/shard_map/all_to_all | solution.py:56
  67.0 3.2 all-to-all-done.6
  70.2 5.5 %all-to-all-start.5 = ((bf16[64,8,512]{2,0,1:T(8,128)(2,1)}), bf16[64,8,512]{2,0,1:T(8,128)(2,1)S(1)}, u32[]{:S(2)}, u32[]{:S(2)}) async-start(bf16[64,8,512]{2,0,1:T(8,128)(2,1)} %bitcast.304), calls=%async_computation.5 | async-start | bytes 1048576 | tf_op jit(solution)/shard_map/all_to_all | solution.py:54
  75.7 2.4 compare_and_fusion
  80.2 70.8 %all-gather.1 = bf16[64,1,4]{2,1,0:T(2,128)(2,1)S(1)} all-gather(bf16[1,1,4]{2,1,0:T(2,128)(2,1)} %get-tuple-element.102), channel_id=1, replica_groups=mesh['ctx'=64,'uly'=8] {'ctx'}, dimensions={0}, use_global_device_ids=true | all-gather | bytes 520 | tf_op jit(solution)/shard_map/all_gather | solution.py:13
  158.9 4.8 %all-to-all-start.1 = ((bf16[64,8,512]{2,0,1:T(8,128)(2,1)}), bf16[64,8,512]{2,0,1:T(8,128)(2,1)S(1)}, u32[]{:S(2)}, u32[]{:S(2)}) async-start(bf16[64,8,512]{2,0,1:T(8,128)(2,1)} %bitcast.307), calls=%async_computation.1 | async-start | bytes 1048576 | tf_op jit(solution)/shard_map/all_to_all | solution.py:50
  163.8 1.8 fusion.6
  165.6 1.8 fusion
  167.4 1.8 fusion.3
  173.1 3.3 collective-permute-done.3
  176.3 2.0 fusion.29
  178.4 2.1 divide_convert_fusion
  182.0 3.5 %fusion.28 = f32[512,4,128]{0,2,1:T(8,128)S(1)} fusion(f32[4,512]{1,0:T(4,128)S(1)} %bitcast.327, pred[512,512]{1,0:T(8,128)(4,1)} %get-tuple-element.111, bf16[512,4,128]{2,1,0:T(4,128)(2,1)} %copy-done.4, f32[512,4,128]{2,1,0:T(4,128)S(1)} %reshape.426, f32[512,4,128]{2,1,0:T(4,128)S(1)} %reshape.427), kind=kOutput, calls=%fused_computation.34 | convolution fusion | flops 545783808 | bytes 3940352 | tf_op jit(solution)/shard_map/hts,shd->thd/dot_general | solution.py:79
  185.4 25.0 %all-gather.4.cloned.1.call-done = bf16[256,128,128]{2,1,0:T(8,128)(2,1)} async-done(((bf16[4,128,128]{2,1,0:T(8,128)(2,1)}), bf16[256,128,128]{2,1,0:T(8,128)(2,1)}) %all-gather.4.cloned.1.call-update) | async-done | bytes 8388624 | tf_op jit(solution)/shard_map/all_gather | solution.py:13
  210.4 107.6 %while.12 = (s32[]{:T(128)}, f32[4,128,128]{2,1,0:T(8,128)S(1)}, s32[]{:T(128)}, bf16[64,4]{1,0:T(8,128)(2,1)}, bf16[64,4,128,128]{3,2,1,0:T(8,128)(2,1)}, /*index=5*/s32[]{:T(128)}, s32[]{:T(128)}, s32[]{:T(128)}) while((s32[]{:T(128)}, f32[4,128,128]{2,1,0:T(8,128)S(1)}, s32[]{:T(128)}, bf16[64,4]{1,0:T(8,128)(2,1)}, ...), condition=%wide.region_5.6_spmd, body=%wide.region_4.5_spmd.sunk | while | flops 196617 | bytes 655527 | solution.py:27
  (216 shorter events, 135.7 us)
Async XLA Ops:
  7.2 42.7 %copy-start = (bf16[64,1024]{1,0:T(8,128)(2,1)S(1)}, bf16[64,1024]{1,0:T(8,128)(2,1)}, u32[]{:S(2)}) copy-start(bf16[64,1024]{1,0:T(8,128)(2,1)} %param.18) | copy-start | bytes 393220
  8.6 12.8 %all-to-all-start = ((bf16[8,2,128]{2,1,0:T(2,128)(2,1)}), bf16[8,2,128]{2,1,0:T(2,128)(2,1)S(1)}, u32[]{:S(2)}, u32[]{:S(2)}) async-start(bf16[8,2,128]{2,1,0:T(2,128)(2,1)} %reshape.440), calls=%async_computation | async-start | bytes 8192 | tf_op jit(solution)/shard_map/all_to_all | solution.py:53
  13.4 8.0 %copy-start.9 = (s32[512]{0:T(512)}, s32[512]{0:T(512)S(1)}, u32[]{:S(2)}) copy-start(s32[512]{0:T(512)S(1)} %get-tuple-element.123) | copy-start | bytes 6148
  13.4 8.0 %copy-start.8 = (s32[512]{0:T(512)}, s32[512]{0:T(512)S(1)}, u32[]{:S(2)}) copy-start(s32[512]{0:T(512)S(1)} %fusion.81) | copy-start | bytes 6148
  21.4 13.1 %all-to-all-start.2 = ((bf16[64,8,512]{2,0,1:T(8,128)(2,1)}), bf16[64,8,512]{2,0,1:T(8,128)(2,1)S(1)}, u32[]{:S(2)}, u32[]{:S(2)}) async-start(bf16[64,8,512]{2,0,1:T(8,128)(2,1)} %bitcast.306), calls=%async_computation.2 | async-start | bytes 1048576 | tf_op jit(solution)/shard_map/all_to_all | solution.py:51
  34.5 13.8 %all-to-all-start.3 = ((bf16[64,8,512]{2,0,1:T(8,128)(2,1)}), bf16[64,8,512]{2,0,1:T(8,128)(2,1)S(1)}, u32[]{:S(2)}, u32[]{:S(2)}) async-start(bf16[64,8,512]{2,0,1:T(8,128)(2,1)} %bitcast.305), calls=%async_computation.3 | async-start | bytes 1048576 | tf_op jit(solution)/shard_map/all_to_all | solution.py:52
  40.0 170.4 %all-gather.4.cloned.1.call-start = ((), (), s32[]{:S(2)}) async-start(), calls=%async_computation.7 | async-start | bytes 8519680 | tf_op jit(solution)/shard_map/all_gather | solution.py:13
  41.5 15.1 %copy-start.7 = (bf16[64,1024]{1,0:T(8,128)(2,1)S(1)}, bf16[64,1024]{1,0:T(8,128)(2,1)}, u32[]{:S(2)}) copy-start(bf16[64,1024]{1,0:T(8,128)(2,1)} %param.19) | copy-start | bytes 393220
  41.5 24.6 %copy-start.2 = (bf16[64,4096]{1,0:T(8,128)(2,1)S(1)}, bf16[64,4096]{1,0:T(8,128)(2,1)}, u32[]{:S(2)}) copy-start(bf16[64,4096]{1,0:T(8,128)(2,1)} %param.17) | copy-start | bytes 1572868
  48.4 21.8 %copy-start.4 = (bf16[512,4,128]{2,1,0:T(4,128)(2,1)}, bf16[512,4,128]{2,1,0:T(4,128)(2,1)S(1)}, u32[]{:S(2)}) copy-start(bf16[512,4,128]{2,1,0:T(4,128)(2,1)S(1)} %reshape.414) | copy-start | bytes 1572868
  49.9 29.5 %copy-start.3 = (bf16[64,4096]{1,0:T(8,128)(2,1)S(1)}, bf16[64,4096]{1,0:T(8,128)(2,1)}, u32[]{:S(2)}) copy-start(bf16[64,4096]{1,0:T(8,128)(2,1)} %param.11) | copy-start | bytes 1572868
  49.9 102.0 %copy-start.1 = (f32[512,4]{1,0:T(8,128)S(1)}, f32[512,4]{1,0:T(8,128)}, u32[]{:S(2)}) copy-start(f32[512,4]{1,0:T(8,128)} %get-tuple-element.100) | copy-start | bytes 24580
  50.6 10.1 %all-to-all-start.4 = ((bf16[64,8,128]{2,0,1:T(8,128)(2,1)}), bf16[64,8,128]{2,0,1:T(8,128)(2,1)}, u32[]{:S(2)}, u32[]{:S(2)}) async-start(bf16[64,8,128]{2,0,1:T(8,128)(2,1)} %copy_bitcast_fusion.5), calls=%async_computation.4 | async-start | bytes 262144 | tf_op jit(solution)/shard_map/all_to_all | solution.py:55
  60.7 9.4 %all-to-all-start.6 = ((bf16[64,8,128]{2,0,1:T(8,128)(2,1)}), bf16[64,8,128]{2,0,1:T(8,128)(2,1)S(1)}, u32[]{:S(2)}, u32[]{:S(2)}) async-start(bf16[64,8,128]{2,0,1:T(8,128)(2,1)} %copy_bitcast_fusion.4), calls=%async_computation.6 | async-start | bytes 262144 | tf_op jit(solution)/shard_map/all_to_all | solution.py:56
  70.2 5.5 %copy-start.5 = (bf16[64,8,128]{2,0,1:T(8,128)(2,1)}, bf16[64,8,128]{2,0,1:T(8,128)(2,1)S(1)}, u32[]{:S(2)}) copy-start(bf16[64,8,128]{2,0,1:T(8,128)(2,1)S(1)} %all-to-all-done.6) | copy-start | bytes 393220
  70.2 88.7 %all-to-all-start.5 = ((bf16[64,8,512]{2,0,1:T(8,128)(2,1)}), bf16[64,8,512]{2,0,1:T(8,128)(2,1)S(1)}, u32[]{:S(2)}, u32[]{:S(2)}) async-start(bf16[64,8,512]{2,0,1:T(8,128)(2,1)} %bitcast.304), calls=%async_computation.5 | async-start | bytes 1048576 | tf_op jit(solution)/shard_map/all_to_all | solution.py:54
  152.0 13.6 %collective-permute-start.2 = (bf16[512,128]{1,0:T(8,128)(2,1)}, bf16[512,128]{1,0:T(8,128)(2,1)}, u32[]{:S(2)}, u32[]{:S(2)}) collective-permute-start(bf16[512,128]{1,0:T(8,128)(2,1)} %bitcast.20), channel_id=1, source_target_pairs={{0,16},{8,24},{16,32},{24,40},{32,48},{40,56},{48,64},{56,72},{64,... | collective-permute-start | bytes 393224 | tf_op jit(solution)/shard_map/ppermute | solution.py:33
  153.3 14.1 %collective-permute-start = (bf16[512,128]{1,0:T(8,128)(2,1)}, bf16[512,128]{1,0:T(8,128)(2,1)}, u32[]{:S(2)}, u32[]{:S(2)}) collective-permute-start(bf16[512,128]{1,0:T(8,128)(2,1)} %bitcast.20), channel_id=1, source_target_pairs={{0,8},{8,16},{16,24},{24,32},{32,40},{40,48},{48,56},{56,64},{64,7... | collective-permute-start | bytes 393224 | tf_op jit(solution)/shard_map/ppermute | solution.py:33
  156.3 20.1 %collective-permute-start.3 = (bf16[512,128]{0,1:T(8,128)(2,1)}, bf16[512,128]{0,1:T(8,128)(2,1)}, u32[]{:S(2)}, u32[]{:S(2)}) collective-permute-start(bf16[512,128]{0,1:T(8,128)(2,1)} %copy.181), channel_id=1, source_target_pairs={{0,16},{8,24},{16,32},{24,40},{32,48},{40,56},{48,64},{56,72},{64,... | collective-permute-start | bytes 393224 | tf_op jit(solution)/shard_map/ppermute | solution.py:33
  157.6 20.8 %collective-permute-start.1 = (bf16[512,128]{0,1:T(8,128)(2,1)}, bf16[512,128]{0,1:T(8,128)(2,1)}, u32[]{:S(2)}, u32[]{:S(2)}) collective-permute-start(bf16[512,128]{0,1:T(8,128)(2,1)} %copy.181), channel_id=1, source_target_pairs={{0,8},{8,16},{16,24},{24,32},{32,40},{40,48},{48,56},{56,64},{64,7... | collective-permute-start | bytes 393224 | tf_op jit(solution)/shard_map/ppermute | solution.py:33
  158.9 22.6 %all-to-all-start.1 = ((bf16[64,8,512]{2,0,1:T(8,128)(2,1)}), bf16[64,8,512]{2,0,1:T(8,128)(2,1)S(1)}, u32[]{:S(2)}, u32[]{:S(2)}) async-start(bf16[64,8,512]{2,0,1:T(8,128)(2,1)} %bitcast.307), calls=%async_computation.1 | async-start | bytes 1048576 | tf_op jit(solution)/shard_map/all_to_all | solution.py:50
  170.2 1.9 copy-start.6
  210.4 108.2 %copy-start.10 = (f32[512]{0:T(512)S(1)}, f32[512]{0:T(512)}, u32[]{:S(2)}) copy-start(f32[512]{0:T(512)} %param.15) | copy-start | bytes 6148
Sparse Core Ops, SparseCore 0:
  50.0 160.3 all-gather.3
where the time goes:
time: 330 us; the launch traced here: 327 us
  other arithmetic  117 us (35%)
  blocking collectives  70.8 us (21%)
  waiting for transfers between devices  47.3 us (14%)
  starting transfers between devices  41.9 us (13%)
  local copies, waits for them, and re-layouts  17 us (5%)
  matrix products  16 us (5%)
  between operations  15 us (5%)
    all_gather x1, blocking collectives, prefix(): lax.all_gather(a.astype(kind), axis)  70.8 us
    add x63, other arithmetic, combine_states(): later_part[0][:, None, None] * earlier[1] + later_part[1]  63.7 us
    convert_element_type x63, other arithmetic, one(): lax.dynamic_index_in_dim(a, turn, 0, False).astype(own.dtype)  42.1 us
    all_gather x1, waiting for transfers between devices, prefix(): lax.all_gather(a.astype(kind), axis)  25 us
    all_to_all x1, waiting for transfers between devices, shards(): lax.all_to_all(lin_value, 'uly', split_axis=1, concat_axis=0, tiled=True)  6.71 us
  transfers between devices with their start and end apart: 12, of which 6 were waited for; matrix products, arithmetic and copies ran while one was open for 12% of the time, Pallas kernels for 0%

commit v1 on v0

--- a/solution.py
+++ b/solution.py
@@ -48,7 +48,12 @@
 ):
     query_in, key_in, value_in, decay_in, att_q, att_k, att_v = (
         lax.all_to_all(lin_query, "uly", split_axis=1, concat_axis=0, tiled=True),
-        lax.all_to_all(lin_key, "uly", split_axis=1, concat_axis=0, tiled=True),
+        jnp.concatenate(
+            lax.all_to_all(
+                jnp.stack(jnp.split(lin_key, lax.axis_size("uly"), axis=1)), "uly", 0, 0
+            ),
+            axis=0,
+        ),
         lax.all_to_all(lin_value, "uly", split_axis=1, concat_axis=0, tiled=True),
         lax.all_to_all(log_decay, "uly", split_axis=1, concat_axis=0, tiled=True),
         lax.all_to_all(att_query, "uly", split_axis=1, concat_axis=0, tiled=True),

time: 330 us -> 343 us (1.039)
  the two profiles are of different devices: /device:TPU:510 before, /device:TPU:504 now
where the time goes in v1:
time: 343 us; the launch traced here: 339 us
  other arithmetic  116 us (34%)
  blocking collectives  70.5 us (21%)
  waiting for transfers between devices  56.6 us (17%)
  starting transfers between devices  33.4 us (10%)
  local copies, waits for them, and re-layouts  27.9 us (8%)
  matrix products  18.2 us (5%)
  between operations  15.2 us (4%)
    all_gather x1, blocking collectives, prefix(): lax.all_gather(a.astype(kind), axis)  70.5 us
    add x63, other arithmetic, combine_states(): later_part[0][:, None, None] * earlier[1] + later_part[1]  63.7 us
    convert_element_type x63, other arithmetic, one(): lax.dynamic_index_in_dim(a, turn, 0, False).astype(own.dtype)  42.5 us
    all_gather x1, waiting for transfers between devices, prefix(): lax.all_gather(a.astype(kind), axis)  24.8 us
    unnamed x40, local copies, waits for them, and re-layouts  13.8 us
    all_to_all x1, waiting for transfers between devices, shards(): lax.all_to_all(jnp.stack(jnp.split(lin_key, lax.axis_size('uly'), axis=1)...  9.18 us
    all_to_all x1, waiting for transfers between devices, shards(): lax.all_to_all(lin_value, 'uly', split_axis=1, concat_axis=0, tiled=True)  8.36 us
  transfers between devices with their start and end apart: 12, of which 6 were waited for; matrix products, arithmetic and copies ran while one was open for 15% of the time, Pallas kernels for 0%

profile of v1, /device:TPU:504, one launch (start us, length us, event | category | flops | bytes accessed | tf_op | source)
XLA Modules:
  0.0 339.0 jit_solution(9923271544291375744)
XLA Ops:
  8.6 4.3 %all-to-all-start = ((bf16[8,2,128]{2,1,0:T(2,128)(2,1)}), bf16[8,2,128]{2,1,0:T(2,128)(2,1)S(1)}, u32[]{:S(2)}, u32[]{:S(2)}) async-start(bf16[8,2,128]{2,1,0:T(2,128)(2,1)} %reshape.435), calls=%async_computation | async-start | bytes 8192 | tf_op jit(solution)/shard_map/all_to_all | solution.py:58
  28.9 1.9 copy.266
  30.8 4.8 %all-to-all-start.3 = ((bf16[64,8,512]{2,0,1:T(8,128)(2,1)}), bf16[64,8,512]{2,0,1:T(8,128)(2,1)S(1)}, u32[]{:S(2)}, u32[]{:S(2)}) async-start(bf16[64,8,512]{2,0,1:T(8,128)(2,1)} %bitcast.316), calls=%async_computation.3 | async-start | bytes 1048576 | tf_op jit(solution)/shard_map/all_to_all | solution.py:57
  37.6 8.4 %all-to-all-done.3 = bf16[64,8,512]{2,0,1:T(8,128)(2,1)S(1)} async-done(((bf16[64,8,512]{2,0,1:T(8,128)(2,1)}), bf16[64,8,512]{2,0,1:T(8,128)(2,1)S(1)}, u32[]{:S(2)}, u32[]{:S(2)}) %all-to-all-start.3) | async-done | bytes 524320 | tf_op jit(solution)/shard_map/all_to_all | solution.py:57
  46.0 3.5 %all-to-all-start.2 = ((bf16[8,64,512]{2,1,0:T(8,128)(2,1)}), bf16[8,64,512]{2,1,0:T(8,128)(2,1)S(1)}, u32[]{:S(2)}, u32[]{:S(2)}) async-start(bf16[8,64,512]{2,1,0:T(8,128)(2,1)} %bitcast_dynamic-update-slice_fusion), calls=%async_computation.2 | async-start | bytes 1048576 | tf_op jit(solution)/shard_map/all_to_all | solution.py:52
  50.5 9.2 %all-to-all-done.2 = bf16[8,64,512]{2,1,0:T(8,128)(2,1)S(1)} async-done(((bf16[8,64,512]{2,1,0:T(8,128)(2,1)}), bf16[8,64,512]{2,1,0:T(8,128)(2,1)S(1)}, u32[]{:S(2)}, u32[]{:S(2)}) %all-to-all-start.2) | async-done | bytes 524320 | tf_op jit(solution)/shard_map/all_to_all | solution.py:52
  62.3 4.0 %all-to-all-start.4 = ((bf16[64,8,128]{2,0,1:T(8,128)(2,1)}), bf16[64,8,128]{2,0,1:T(8,128)(2,1)}, u32[]{:S(2)}, u32[]{:S(2)}) async-start(bf16[64,8,128]{2,0,1:T(8,128)(2,1)} %copy_bitcast_fusion.4), calls=%async_computation.4 | async-start | bytes 262144 | tf_op jit(solution)/shard_map/all_to_all | solution.py:60
  67.0 5.4 %all-to-all-done.4 = bf16[64,8,128]{2,0,1:T(8,128)(2,1)} async-done(((bf16[64,8,128]{2,0,1:T(8,128)(2,1)}), bf16[64,8,128]{2,0,1:T(8,128)(2,1)}, u32[]{:S(2)}, u32[]{:S(2)}) %all-to-all-start.4) | async-done | bytes 131104 | tf_op jit(solution)/shard_map/all_to_all | solution.py:60
  72.4 3.4 all-to-all-start.6
  76.7 5.2 %all-to-all-done.6 = bf16[64,8,128]{2,0,1:T(8,128)(2,1)S(1)} async-done(((bf16[64,8,128]{2,0,1:T(8,128)(2,1)}), bf16[64,8,128]{2,0,1:T(8,128)(2,1)S(1)}, u32[]{:S(2)}, u32[]{:S(2)}) %all-to-all-start.6) | async-done | bytes 131104 | tf_op jit(solution)/shard_map/all_to_all | solution.py:61
  81.8 3.5 %all-to-all-start.5 = ((bf16[64,8,512]{2,0,1:T(8,128)(2,1)}), bf16[64,8,512]{2,0,1:T(8,128)(2,1)S(1)}, u32[]{:S(2)}, u32[]{:S(2)}) async-start(bf16[64,8,512]{2,0,1:T(8,128)(2,1)} %bitcast.315), calls=%async_computation.5 | async-start | bytes 1048576 | tf_op jit(solution)/shard_map/all_to_all | solution.py:59
  88.4 1.9 copy.267
  90.3 70.5 %all-gather.1 = bf16[64,1,4]{2,1,0:T(2,128)(2,1)S(1)} all-gather(bf16[1,1,4]{2,1,0:T(2,128)(2,1)} %get-tuple-element.109), channel_id=1, replica_groups=mesh['ctx'=64,'uly'=8] {'ctx'}, dimensions={0}, use_global_device_ids=true | all-gather | bytes 520 | tf_op jit(solution)/shard_map/all_gather | solution.py:13
  168.6 4.7 %all-to-all-start.1 = ((bf16[64,8,512]{2,0,1:T(8,128)(2,1)}), bf16[64,8,512]{2,0,1:T(8,128)(2,1)S(1)}, u32[]{:S(2)}, u32[]{:S(2)}) async-start(bf16[64,8,512]{2,0,1:T(8,128)(2,1)} %bitcast.317), calls=%async_computation.1 | async-start | bytes 1048576 | tf_op jit(solution)/shard_map/all_to_all | solution.py:50
  173.4 1.8 fusion.6
  175.2 1.8 fusion
  177.0 1.8 fusion.3
  182.7 3.6 %collective-permute-done.3 = bf16[512,128]{0,1:T(8,128)(2,1)} collective-permute-done((bf16[512,128]{0,1:T(8,128)(2,1)}, bf16[512,128]{0,1:T(8,128)(2,1)}, u32[]{:S(2)}, u32[]{:S(2)}) %collective-permute-start.3) | collective-permute-done | bytes 131104 | tf_op jit(solution)/shard_map/ppermute | solution.py:33
  186.3 2.0 fusion.29
  188.3 2.1 divide_convert_fusion
  192.0 4.4 %fusion.28 = f32[512,4,128]{0,2,1:T(8,128)} fusion(f32[4,512]{1,0:T(4,128)S(1)} %bitcast.336, pred[512,512]{1,0:T(8,128)(4,1)S(1)} %copy-done.5, bf16[512,4,128]{2,1,0:T(4,128)(2,1)} %copy-done.2, f32[512,4,128]{2,1,0:T(4,128)S(1)} %reshape.421, f32[512,4,128]{2,1,0:T(4,128)S(1)} %reshape.422), kind=kOutput, calls=%fused_computation.34 | convolution fusion | flops 545783808 | bytes 3940352 | tf_op jit(solution)/shard_map/hts,shd->thd/dot_general | solution.py:84
  196.4 24.8 %all-gather.4.cloned.1.call-done = bf16[256,128,128]{2,1,0:T(8,128)(2,1)} async-done(((bf16[4,128,128]{2,1,0:T(8,128)(2,1)}), bf16[256,128,128]{2,1,0:T(8,128)(2,1)}) %all-gather.4.cloned.1.call-update) | async-done | bytes 8388624 | tf_op jit(solution)/shard_map/all_gather | solution.py:13
  221.2 108.0 %while.12 = (s32[]{:T(128)}, f32[4,128,128]{2,1,0:T(8,128)S(1)}, s32[]{:T(128)}, bf16[64,4]{1,0:T(8,128)(2,1)}, bf16[64,4,128,128]{3,2,1,0:T(8,128)(2,1)}, /*index=5*/s32[]{:T(128)}, s32[]{:T(128)}, s32[]{:T(128)}) while((s32[]{:T(128)}, f32[4,128,128]{2,1,0:T(8,128)S(1)}, s32[]{:T(128)}, bf16[64,4]{1,0:T(8,128)(2,1)}, ...), condition=%wide.region_5.6_spmd, body=%wide.region_4.5_spmd.sunk | while | flops 196617 | bytes 655527 | solution.py:27
  329.2 1.8 multiply_reduce_fusion
  (228 shorter events, 147.3 us)
Async XLA Ops:
  7.2 54.4 %copy-start = (bf16[64,1024]{1,0:T(8,128)(2,1)S(1)}, bf16[64,1024]{1,0:T(8,128)(2,1)}, u32[]{:S(2)}) copy-start(bf16[64,1024]{1,0:T(8,128)(2,1)} %param.18) | copy-start | bytes 393220
  8.6 22.2 %all-to-all-start = ((bf16[8,2,128]{2,1,0:T(2,128)(2,1)}), bf16[8,2,128]{2,1,0:T(2,128)(2,1)S(1)}, u32[]{:S(2)}, u32[]{:S(2)}) async-start(bf16[8,2,128]{2,1,0:T(2,128)(2,1)} %reshape.435), calls=%async_computation | async-start | bytes 8192 | tf_op jit(solution)/shard_map/all_to_all | solution.py:58
  12.9 33.1 %copy-start.9 = (s32[512]{0:T(512)}, s32[512]{0:T(512)S(1)}, u32[]{:S(2)}) copy-start(s32[512]{0:T(512)S(1)} %get-tuple-element.130) | copy-start | bytes 6148
  12.9 33.0 %copy-start.7 = (s32[512]{0:T(512)}, s32[512]{0:T(512)S(1)}, u32[]{:S(2)}) copy-start(s32[512]{0:T(512)S(1)} %fusion.81) | copy-start | bytes 6148
  30.8 15.1 %all-to-all-start.3 = ((bf16[64,8,512]{2,0,1:T(8,128)(2,1)}), bf16[64,8,512]{2,0,1:T(8,128)(2,1)S(1)}, u32[]{:S(2)}, u32[]{:S(2)}) async-start(bf16[64,8,512]{2,0,1:T(8,128)(2,1)} %bitcast.316), calls=%async_computation.3 | async-start | bytes 1048576 | tf_op jit(solution)/shard_map/all_to_all | solution.py:57
  46.0 13.8 %all-to-all-start.2 = ((bf16[8,64,512]{2,1,0:T(8,128)(2,1)}), bf16[8,64,512]{2,1,0:T(8,128)(2,1)S(1)}, u32[]{:S(2)}, u32[]{:S(2)}) async-start(bf16[8,64,512]{2,1,0:T(8,128)(2,1)} %bitcast_dynamic-update-slice_fusion), calls=%async_computation.2 | async-start | bytes 1048576 | tf_op jit(solution)/shard_map/all_to_all | solution.py:52
  49.5 171.7 %all-gather.4.cloned.1.call-start = ((), (), s32[]{:S(2)}) async-start(), calls=%async_computation.7 | async-start | bytes 8519680 | tf_op jit(solution)/shard_map/all_gather | solution.py:13
  50.5 31.3 %copy-start.2 = (bf16[512,4,128]{2,1,0:T(4,128)(2,1)}, bf16[512,4,128]{2,1,0:T(4,128)(2,1)S(1)}, u32[]{:S(2)}) copy-start(bf16[512,4,128]{2,1,0:T(4,128)(2,1)S(1)} %reshape.409) | copy-start | bytes 1572868
  50.5 15.8 %copy-start.6 = (bf16[64,1024]{1,0:T(8,128)(2,1)S(1)}, bf16[64,1024]{1,0:T(8,128)(2,1)}, u32[]{:S(2)}) copy-start(bf16[64,1024]{1,0:T(8,128)(2,1)} %param.19) | copy-start | bytes 393220
  50.5 25.3 %copy-start.1 = (bf16[64,4096]{1,0:T(8,128)(2,1)S(1)}, bf16[64,4096]{1,0:T(8,128)(2,1)}, u32[]{:S(2)}) copy-start(bf16[64,4096]{1,0:T(8,128)(2,1)} %param.17) | copy-start | bytes 1572868
  60.1 25.3 %copy-start.8 = (s32[512]{0:T(512)S(1)}, s32[512]{0:T(512)}, u32[]{:S(2)}) copy-start(s32[512]{0:T(512)} %copy-done.7) | copy-start | bytes 6148
  60.1 25.3 %copy-start.10 = (s32[512]{0:T(512)S(1)}, s32[512]{0:T(512)}, u32[]{:S(2)}) copy-start(s32[512]{0:T(512)} %copy-done.9) | copy-start | bytes 6148
  60.1 25.3 %copy-start.11 = (s32[512]{0:T(512)S(1)}, s32[512]{0:T(512)}, u32[]{:S(2)}) copy-start(s32[512]{0:T(512)} %get-tuple-element.91) | copy-start | bytes 6148
  60.1 25.3 %copy-start.12 = (s32[512]{0:T(512)S(1)}, s32[512]{0:T(512)}, u32[]{:S(2)}) copy-start(s32[512]{0:T(512)} %get-tuple-element.93) | copy-start | bytes 6148
  62.3 10.1 %all-to-all-start.4 = ((bf16[64,8,128]{2,0,1:T(8,128)(2,1)}), bf16[64,8,128]{2,0,1:T(8,128)(2,1)}, u32[]{:S(2)}, u32[]{:S(2)}) async-start(bf16[64,8,128]{2,0,1:T(8,128)(2,1)} %copy_bitcast_fusion.4), calls=%async_computation.4 | async-start | bytes 262144 | tf_op jit(solution)/shard_map/all_to_all | solution.py:60
  72.4 9.4 %all-to-all-start.6 = ((bf16[64,8,128]{2,0,1:T(8,128)(2,1)}), bf16[64,8,128]{2,0,1:T(8,128)(2,1)S(1)}, u32[]{:S(2)}, u32[]{:S(2)}) async-start(bf16[64,8,128]{2,0,1:T(8,128)(2,1)} %copy_bitcast_fusion.3), calls=%async_computation.6 | async-start | bytes 262144 | tf_op jit(solution)/shard_map/all_to_all | solution.py:61
  81.8 6.1 %copy-start.3 = (bf16[64,8,128]{2,0,1:T(8,128)(2,1)}, bf16[64,8,128]{2,0,1:T(8,128)(2,1)S(1)}, u32[]{:S(2)}) copy-start(bf16[64,8,128]{2,0,1:T(8,128)(2,1)S(1)} %all-to-all-done.6) | copy-start | bytes 393220
  81.8 86.7 %all-to-all-start.5 = ((bf16[64,8,512]{2,0,1:T(8,128)(2,1)}), bf16[64,8,512]{2,0,1:T(8,128)(2,1)S(1)}, u32[]{:S(2)}, u32[]{:S(2)}) async-start(bf16[64,8,512]{2,0,1:T(8,128)(2,1)} %bitcast.315), calls=%async_computation.5 | async-start | bytes 1048576 | tf_op jit(solution)/shard_map/all_to_all | solution.py:59
  161.7 13.5 %collective-permute-start.2 = (bf16[512,128]{1,0:T(8,128)(2,1)}, bf16[512,128]{1,0:T(8,128)(2,1)}, u32[]{:S(2)}, u32[]{:S(2)}) collective-permute-start(bf16[512,128]{1,0:T(8,128)(2,1)} %bitcast.27), channel_id=1, source_target_pairs={{0,16},{8,24},{16,32},{24,40},{32,48},{40,56},{48,64},{56,72},{64,... | collective-permute-start | bytes 393224 | tf_op jit(solution)/shard_map/ppermute | solution.py:33
  163.0 14.0 %collective-permute-start = (bf16[512,128]{1,0:T(8,128)(2,1)}, bf16[512,128]{1,0:T(8,128)(2,1)}, u32[]{:S(2)}, u32[]{:S(2)}) collective-permute-start(bf16[512,128]{1,0:T(8,128)(2,1)} %bitcast.27), channel_id=1, source_target_pairs={{0,8},{8,16},{16,24},{24,32},{32,40},{40,48},{48,56},{56,64},{64,7... | collective-permute-start | bytes 393224 | tf_op jit(solution)/shard_map/ppermute | solution.py:33
  166.0 20.3 %collective-permute-start.3 = (bf16[512,128]{0,1:T(8,128)(2,1)}, bf16[512,128]{0,1:T(8,128)(2,1)}, u32[]{:S(2)}, u32[]{:S(2)}) collective-permute-start(bf16[512,128]{0,1:T(8,128)(2,1)} %copy.210), channel_id=1, source_target_pairs={{0,16},{8,24},{16,32},{24,40},{32,48},{40,56},{48,64},{56,72},{64,... | collective-permute-start | bytes 393224 | tf_op jit(solution)/shard_map/ppermute | solution.py:33
  167.2 21.1 %collective-permute-start.1 = (bf16[512,128]{0,1:T(8,128)(2,1)}, bf16[512,128]{0,1:T(8,128)(2,1)}, u32[]{:S(2)}, u32[]{:S(2)}) collective-permute-start(bf16[512,128]{0,1:T(8,128)(2,1)} %copy.210), channel_id=1, source_target_pairs={{0,8},{8,16},{16,24},{24,32},{32,40},{40,48},{48,56},{56,64},{64,7... | collective-permute-start | bytes 393224 | tf_op jit(solution)/shard_map/ppermute | solution.py:33
  168.6 22.9 %all-to-all-start.1 = ((bf16[64,8,512]{2,0,1:T(8,128)(2,1)}), bf16[64,8,512]{2,0,1:T(8,128)(2,1)S(1)}, u32[]{:S(2)}, u32[]{:S(2)}) async-start(bf16[64,8,512]{2,0,1:T(8,128)(2,1)} %bitcast.317), calls=%async_computation.1 | async-start | bytes 1048576 | tf_op jit(solution)/shard_map/all_to_all | solution.py:50
  221.2 109.8 %copy-start.13 = (f32[512]{0:T(512)S(1)}, f32[512]{0:T(512)}, u32[]{:S(2)}) copy-start(f32[512]{0:T(512)} %param.15) | copy-start | bytes 6148
  (2 other events, 3.4 us)
Sparse Core Ops, SparseCore 0:
  61.7 159.4 all-gather.3
